TPU v7x, 128 devices: a whole 4x4x4 slice. The times are simulated.
128 devices in a mesh: ctx: 8 (over x, y_lo), ch: 16 (over z, y_hi, core).
Axes of the slice: x: 4, y: 4 (y_hi: 2, y_lo: 2; y = y_hi * 2 + y_lo), z: 4, core: 2. Of those that a mesh axis runs over, the one named last changes fastest.
Arguments:
- tokens: bfloat16 [4096, 8192], P('ctx', 'ch'), may hold values from -6 to 6
- proj_value: bfloat16 [8192, 8192], P(None, 'ch'), may hold values from -0.0625 to 0.0625
- proj_gate: bfloat16 [8192, 8192], P(None, 'ch'), may hold values from -0.0625 to 0.0625
- conv_filter: bfloat16 [8192, 4096], P('ch', 'ctx'), may hold values from -4 to 4
- proj_output: bfloat16 [8192, 8192], P('ch'), may hold values from -0.0625 to 0.0625
Outputs:
- mixed: bfloat16 [4096, 8192], P('ctx', 'ch')
All inputs are finite; a program needn't handle non-finite values.
Results may differ from a plain program's by a relative error of at most 0.024.
Values may be sent and summed in bfloat16 or wider, within the bound.
A program may use at most 128 MiB of HBM per device.

v0:
```python
import math

import jax
import jax.numpy as jnp
from jax import lax
from jax.sharding import PartitionSpec as P


def angle_table(first, second, period):
    left = jnp.arange(first, dtype=jnp.int32)[:, None]
    right = jnp.arange(second, dtype=jnp.int32)[None, :]
    angles = -2.0 * math.pi / period * (left * right % period).astype(jnp.float32)
    return (jnp.cos(angles), jnp.sin(angles))


def convolve(values, filters):
    precise = lax.Precision.HIGH
    channels = values.shape[0]
    length = values.shape[1]
    period = 2 * length
    outer_size = 1
    while outer_size * 2 * (outer_size * 2) <= period and period % (outer_size * 2) == 0:
        outer_size = outer_size * 2
    inner_size = period // outer_size
    half_outer = outer_size // 2
    first_cos, first_sin = angle_table(outer_size, outer_size, outer_size)
    second_cos, second_sin = angle_table(inner_size, inner_size, inner_size)
    twist_cos, twist_sin = angle_table(outer_size, inner_size, period)

    def forward(signal):
        folded = signal.astype(jnp.float32).reshape(channels, half_outer, inner_size)
        first_re = jnp.einsum("kn,cnq->ckq", first_cos[:, :half_outer], folded, precision=precise)
        first_im = jnp.einsum("kn,cnq->ckq", first_sin[:, :half_outer], folded, precision=precise)
        turned_re = first_re * twist_cos - first_im * twist_sin
        turned_im = first_re * twist_sin + first_im * twist_cos
        out_re = jnp.einsum("ckq,qm->ckm", turned_re, second_cos, precision=precise) - jnp.einsum(
            "ckq,qm->ckm", turned_im, second_sin, precision=precise
        )
        out_im = jnp.einsum("ckq,qm->ckm", turned_re, second_sin, precision=precise) + jnp.einsum(
            "ckq,qm->ckm", turned_im, second_cos, precision=precise
        )
        return (out_re, out_im)

    value_re, value_im = forward(values)
    filter_re, filter_im = forward(filters)
    product_re = value_re * filter_re - value_im * filter_im
    product_im = value_re * filter_im + value_im * filter_re
    back_re = jnp.einsum("ckq,qm->ckm", product_re, second_cos, precision=precise) + jnp.einsum(
        "ckq,qm->ckm", product_im, second_sin, precision=precise
    )
    back_im = jnp.einsum("ckq,qm->ckm", product_im, second_cos, precision=precise) - jnp.einsum(
        "ckq,qm->ckm", product_re, second_sin, precision=precise
    )
    turned_re = back_re * twist_cos + back_im * twist_sin
    turned_im = back_im * twist_cos - back_re * twist_sin
    signal = jnp.einsum(
        "bk,cka->cba", first_cos[:half_outer], turned_re, precision=precise
    ) + jnp.einsum("bk,cka->cba", first_sin[:half_outer], turned_im, precision=precise)
    return signal.reshape(channels, length) / period


def on_device(tokens, proj_value, proj_gate, conv_filter, proj_output):
    contract = (((0,), (1,)), ((), ()))
    segment = lax.all_gather(tokens, "ch", axis=1, tiled=True)
    value_sum = lax.dot_general(proj_value, segment, contract, preferred_element_type=jnp.float32)
    gate_sum = lax.dot_general(proj_gate, segment, contract, preferred_element_type=jnp.float32)
    value_sum, gate_sum = (value_sum, gate_sum)
    value_local = value_sum.astype(jnp.bfloat16)
    gate_local = gate_sum.astype(jnp.bfloat16)
    value_major, filter_major = (
        lax.all_to_all(value_local, "ctx", split_axis=0, concat_axis=1, tiled=True),
        lax.all_to_all(conv_filter, "ctx", split_axis=0, concat_axis=1, tiled=True),
    )
    result_major = convolve(value_major, filter_major)
    result_local = lax.all_to_all(
        result_major.astype(jnp.bfloat16), "ctx", split_axis=1, concat_axis=0, tiled=True
    ).astype(result_major.dtype)
    gated_local = (result_local * gate_local.astype(jnp.float32)).astype(jnp.bfloat16)
    partial_terms = lax.dot_general(
        gated_local, proj_output, (((0,), (0,)), ((), ())), preferred_element_type=jnp.float32
    )
    return lax.psum_scatter(
        partial_terms.astype(jnp.bfloat16), "ch", scatter_dimension=1, tiled=True
    )


def solution(mesh):
    in_specs = (P("ctx", "ch"), P(None, "ch"), P(None, "ch"), P("ch", "ctx"), P("ch", None))
    out_specs = P("ctx", "ch")
    return jax.shard_map(
        on_device, mesh=mesh, in_specs=in_specs, out_specs=out_specs, check_vma=False
    )
```

profile of v0, /device:TPU:1, one launch (start us, length us, event | category | flops | bytes accessed | tf_op | source)
XLA Modules:
  0.0 267.2 jit_solution(14146387135504426315)
XLA Ops:
  6.5 0.0 all-gather.2.cloned.1.call-start
  6.5 0.7 all-gather.2.cloned.1.call-update
  7.3 5.9 %all-to-all-start.1 = ((bf16[8,64,512]{2,1,0:T(8,128)(2,1)}), bf16[8,64,512]{2,1,0:T(8,128)(2,1)S(1)}, u32[]{:S(2)}, u32[]{:S(2)}) async-start(bf16[8,64,512]{2,1,0:T(8,128)(2,1)} %bitcast.110), calls=%async_computation.1 | async-start | bytes 1048576 | tf_op jit(solution)/shard_map/all_to_all | solution.py:72
  13.1 0.1 fusion.98
  13.3 0.1 fusion.97
  13.4 0.1 fusion.95
  13.6 8.3 %all-to-all-done.1 = bf16[8,64,512]{2,1,0:T(8,128)(2,1)S(1)} async-done(((bf16[8,64,512]{2,1,0:T(8,128)(2,1)}), bf16[8,64,512]{2,1,0:T(8,128)(2,1)S(1)}, u32[]{:S(2)}, u32[]{:S(2)}) %all-to-all-start.1) | async-done | bytes 524320 | tf_op jit(solution)/shard_map/all_to_all | solution.py:72
  21.8 0.3 copy.16
  22.1 0.3 reshape.61
  22.4 0.8 fusion.101
  23.2 0.8 fusion.99
  24.0 0.0 copy-start
  24.0 1.3 fusion
  25.3 0.0 copy-done
  25.3 2.8 %fusion.21 = f32[64,64,128]{2,1,0:T(8,128)} fusion(f32[64,64,128]{2,1,0:T(8,128)S(1)} %fusion, f32[64,64,128]{2,0,1:T(8,128)S(1)} %fusion.101, f32[64,64,128]{2,0,1:T(8,128)S(1)} %fusion.99, f32[64,128]{1,0:T(8,128)S(1)} %get-tuple-element.7, f32[64,128]{1,0:T(8,128)S(1)} %get-tuple-element.8), kind=kOutput, calls=%fused_computation.28 | convolution fusion | flops 404979712 | bytes 8454144 | tf_op jit(solution)/shard_map/ckq,qm->ckm/dot_general | solution.py:39
  28.1 62.5 %all-gather.2.cloned.1.call-done = bf16[512,8192]{1,0:T(8,128)(2,1)} async-done(((bf16[512,512]{1,0:T(8,128)(2,1)}), bf16[512,8192]{1,0:T(8,128)(2,1)}) %all-gather.2.cloned.1.call-update) | async-done | bytes 8388624 | tf_op jit(solution)/shard_map/all_gather | solution.py:64
  90.6 11.1 %convolution_convert_fusion.2 = bf16[512,512]{1,0:T(8,128)(2,1)} fusion(bf16[8192,512]{1,0:T(8,128)(2,1)} %param.6, bf16[512,8192]{1,0:T(8,128)(2,1)} %all-gather.2.cloned.1.call-done), kind=kOutput, calls=%fused_computation.40 | convolution fusion | flops 4295229440 | bytes 17301504 | tf_op jit(solution)/shard_map/dot_general | solution.py:65
  101.7 4.0 %all-to-all-start = ((bf16[8,64,512]{2,1,0:T(8,128)(2,1)}), bf16[8,64,512]{2,1,0:T(8,128)(2,1)S(1)}, u32[]{:S(2)}, u32[]{:S(2)}) async-start(bf16[8,64,512]{2,1,0:T(8,128)(2,1)} %bitcast), calls=%async_computation | async-start | bytes 1048576 | tf_op jit(solution)/shard_map/all_to_all | solution.py:71
  105.7 0.2 reduce-scatter.2.cloned.1.call-start
  106.0 0.0 copy-start.1
  106.0 3.0 %fusion.2 = f32[64,64,128]{2,1,0:T(8,128)S(1)} fusion(f32[64,64,128]{2,0,1:T(8,128)S(1)} %fusion.101, f32[64,64,128]{2,0,1:T(8,128)} %copy-done, f32[64,128]{1,0:T(8,128)S(1)} %get-tuple-element.7, f32[64,128]{1,0:T(8,128)S(1)} %get-tuple-element.8), kind=kOutput, calls=%fused_computation.3 | convolution fusion | flops 404455424 | bytes 6356992 | tf_op jit(solution)/shard_map/ckq,qm->ckm/dot_general | solution.py:36
  109.0 0.0 copy-done.1
  109.0 2.7 %fusion.18 = f32[64,64,128]{2,1,0:T(8,128)} fusion(f32[64,64,128]{2,1,0:T(8,128)S(1)} %fusion.2, f32[64,64,128]{2,0,1:T(8,128)S(1)} %fusion.101, f32[64,64,128]{2,0,1:T(8,128)S(1)} %copy-done.1, f32[64,128]{1,0:T(8,128)S(1)} %get-tuple-element.7, f32[64,128]{1,0:T(8,128)S(1)} %get-tuple-element.8), kind=kOutput, calls=%fused_computation.27 | convolution fusion | flops 404979712 | bytes 8454144 | tf_op jit(solution)/shard_map/ckq,qm->ckm/dot_general | solution.py:36
  111.8 3.1 %all-to-all-done = bf16[8,64,512]{2,1,0:T(8,128)(2,1)S(1)} async-done(((bf16[8,64,512]{2,1,0:T(8,128)(2,1)}), bf16[8,64,512]{2,1,0:T(8,128)(2,1)S(1)}, u32[]{:S(2)}, u32[]{:S(2)}) %all-to-all-start) | async-done | bytes 524320 | tf_op jit(solution)/shard_map/all_to_all | solution.py:71
  114.9 0.3 copy.15
  115.2 0.3 reshape.60
  115.5 0.8 fusion.102
  116.3 0.8 fusion.100
  117.0 1.3 fusion.45
  118.4 1.3 fusion.47
  119.7 0.0 copy-start.2
  119.7 0.0 copy-start.3
  119.7 1.4 convolution_subtract_fusion.1
  121.1 0.2 copy-done.2
  121.3 0.6 copy-done.3
  121.9 1.7 multiply_add_fusion
  123.7 1.2 fusion.58
  124.9 1.5 fusion.60
  126.4 1.2 convolution_subtract_fusion
  127.6 1.2 convolution_add_fusion
  128.9 0.8 fusion.10
  129.7 0.9 fusion.36
  130.6 0.3 convert_element_type.112
  131.0 0.2 copy.19
  131.1 0.0 slice-start
  131.1 11.2 %all_to_all.42 = bf16[64,8,512]{2,0,1:T(8,128)(2,1)S(1)} all-to-all(bf16[64,8,512]{2,0,1:T(8,128)(2,1)S(1)} %copy.19), channel_id=1, replica_groups=mesh['ctx'=8,'ch'=16] {'ctx'}, dimensions={1} | all-to-all | bytes 1048576 | tf_op jit(solution)/shard_map/all_to_all | solution.py:75
  142.4 0.1 convert_element_type.121
  142.5 0.0 slice-start.1
  142.5 10.5 %fusion.35 = bf16[512,512]{1,0:T(8,128)(2,1)S(1)} fusion(f32[512,512]{1,0:T(8,128)S(1)} %bitcast.109, bf16[8192,512]{1,0:T(8,128)(2,1)} %param.7, bf16[512,8192]{1,0:T(8,128)(2,1)} %all-gather.2.cloned.1.call-done), kind=kOutput, calls=%fused_computation.39 | convolution fusion | flops 4296015872 | bytes 18350080 | tf_op jit(solution)/shard_map/dot_general | solution.py:66
  153.0 0.0 slice-done
  153.0 0.0 slice-done.1
  153.0 6.9 %convolution_convert_fusion = bf16[512,8192]{1,0:T(8,128)(2,1)} fusion(bf16[512,512]{1,0:T(8,128)(2,1)S(1)} %fusion.35, bf16[512,8192]{1,0:T(8,128)(2,1)S(1)} %bitcast.106), kind=kOutput, calls=%fused_computation | convolution fusion | flops 4299161600 | bytes 17301504 | tf_op jit(solution)/shard_map/dot_general | solution.py:79
  159.9 0.0 reduce-scatter.2.cloned.1.call-update
  159.9 100.4 %reduce-scatter.2.cloned.1.call-done = bf16[512,512]{1,0:T(8,128)(2,1)} async-done(((bf16[512,8192]{1,0:T(8,128)(2,1)}), bf16[512,512]{1,0:T(8,128)(2,1)}) %reduce-scatter.2.cloned.1.call-update) | async-done | bytes 524304 | tf_op jit(solution)/shard_map/reduce_scatter | solution.py:82
  (1 shorter events, 0.0 us)
Async XLA Ops:
  6.5 84.1 %all-gather.2.cloned.1.call-start = ((), (), s32[]{:S(2)}) async-start(), calls=%async_computation.4 | async-start | bytes 8912896 | tf_op jit(solution)/shard_map/all_gather | solution.py:64
  7.3 14.6 %all-to-all-start.1 = ((bf16[8,64,512]{2,1,0:T(8,128)(2,1)}), bf16[8,64,512]{2,1,0:T(8,128)(2,1)S(1)}, u32[]{:S(2)}, u32[]{:S(2)}) async-start(bf16[8,64,512]{2,1,0:T(8,128)(2,1)} %bitcast.110), calls=%async_computation.1 | async-start | bytes 1048576 | tf_op jit(solution)/shard_map/all_to_all | solution.py:72
  24.0 1.4 copy-start
  101.7 13.1 %all-to-all-start = ((bf16[8,64,512]{2,1,0:T(8,128)(2,1)}), bf16[8,64,512]{2,1,0:T(8,128)(2,1)S(1)}, u32[]{:S(2)}, u32[]{:S(2)}) async-start(bf16[8,64,512]{2,1,0:T(8,128)(2,1)} %bitcast), calls=%async_computation | async-start | bytes 1048576 | tf_op jit(solution)/shard_map/all_to_all | solution.py:71
  105.7 154.6 %reduce-scatter.2.cloned.1.call-start = ((), (), s32[]{:S(2)}) async-start(), calls=%async_computation.5 | async-start | bytes 8912896 | tf_op jit(solution)/shard_map/reduce_scatter | solution.py:82
  106.0 3.1 %copy-start.1 = (f32[64,64,128]{2,0,1:T(8,128)S(1)}, f32[64,64,128]{2,0,1:T(8,128)}, u32[]{:S(2)}) copy-start(f32[64,64,128]{2,0,1:T(8,128)} %copy-done) | copy-start | bytes 6291460
  119.7 1.6 copy-start.2
  119.7 2.2 copy-start.3
  131.1 21.8 %slice-start = ((s8[8388608]{0:T(1024)(128)(4,1)}), s8[4194304]{0:T(1024)(128)(4,1)S(1)}, s32[]{:S(2)}) async-start(s8[8388608]{0:T(1024)(128)(4,1)} %bitcast.105), calls=%async_computation.6 | async-start | bytes 8388608
  142.5 10.5 %slice-start.1 = ((s8[8388608]{0:T(1024)(128)(4,1)}), s8[4194304]{0:T(1024)(128)(4,1)S(1)}, s32[]{:S(2)}) async-start(s8[8388608]{0:T(1024)(128)(4,1)} %bitcast.105), calls=%async_computation.7 | async-start | bytes 8388608
Sparse Core Ops, SparseCore 0:
  9.7 80.8 all-gather.1
  160.0 100.2 reduce-scatter.1
where the time goes:
time: 268 us; the launch traced here: 267 us
  waiting for transfers between devices  175 us (65%)
  matrix products  54 us (20%)
  between operations  13.7 us (5%)
  blocking collectives  11.2 us (4%)
  starting transfers between devices  10.1 us (4%)
    reduce_scatter x1, waiting for transfers between devices, on_device(): lax.psum_scatter(partial_terms.astype(jnp.bfloat16), 'ch', scatter_dimens...  100 us
    all_gather x1, waiting for transfers between devices, on_device(): segment = lax.all_gather(tokens, 'ch', axis=1, tiled=True)  62.5 us
    all_to_all x1, blocking collectives, on_device(): lax.all_to_all(result_major.astype(jnp.bfloat16), 'ctx', split_axis=1, co...  11.2 us
    dot_general x1, matrix products, on_device(): lax.dot_general(proj_value, segment, contract, preferred_element_type=jnp...  11.1 us
    dot_general x1, matrix products, on_device(): lax.dot_general(proj_gate, segment, contract, preferred_element_type=jnp....  10.5 us
    all_to_all x1, waiting for transfers between devices, on_device(): lax.all_to_all(conv_filter, 'ctx', split_axis=0, concat_axis=1, tiled=True)  8.26 us
    dot_general x1, matrix products, on_device(): lax.dot_general(gated_local, proj_output, (((0,), (0,)), ((), ())), prefe...  6.88 us
    all_to_all x1, starting transfers between devices, on_device(): lax.all_to_all(conv_filter, 'ctx', split_axis=0, concat_axis=1, tiled=True)  5.87 us
  transfers between devices with their start and end apart: 4, of which 4 were waited for; matrix products, arithmetic and copies ran while one was open for 5% of the time, Pallas kernels for 0%

commit v1 on v0

v1 whole, which is shorter than its diff:
```python
import math

import jax
import jax.numpy as jnp
import numpy as np
from jax import lax
from jax.experimental import pallas as pl
from jax.experimental.pallas import tpu as pltpu
from jax.sharding import PartitionSpec as P

MESH = pl.DeviceIdType.MESH
BF16 = jnp.bfloat16
F32 = jnp.float32
N = 512
CTX = 8
CHIPS = 8
HALF = 256
A0, A1, A, B0, B1, B, ALL = (
    (0, 112),
    (112, 112),
    (0, 224),
    (224, 144),
    (368, 144),
    (224, 288),
    (0, 512),
)
TRANSFERS = 128


def tables():
    k = np.arange(HALF)[:, None]
    n = np.arange(2 * HALF)[None, :]
    angle = math.pi / (2 * HALF) * ((2 * k + 1) * n % (4 * HALF))
    forward = np.concatenate([np.cos(angle), -np.sin(angle)], axis=0)
    inverse = forward[:, HALF:].T * (1.0 / HALF)
    return forward.astype(jnp.bfloat16), inverse.astype(jnp.bfloat16)


def dot(a, b):
    return jnp.dot(a, b, preferred_element_type=F32)


def rows_of(part):
    return pl.ds(part[0], part[1])


def swap(x):
    return pltpu.roll(x, 64, axis=1)


def low_lanes(rows):
    return lax.broadcasted_iota(jnp.int32, (rows, 128), 1) < 64


def kernel(
    tok_hbm, wv_hbm, wg_hbm, filt_hbm, wo_hbm, fwd_hbm, inv_hbm, out_ref,
    G, WV, WG, WO, FWD, INV, TF, acc_v, acc_g, VS, HSND, XR, HR, YS, YR,
    XQ, HQ, XS, HS, YP, GA, GB, RYA, RYB, RP, RM, ss, rs, ls,
):
    ctx = lax.axis_index("ctx")
    ch = lax.axis_index("ch")
    z, yh, c = ch // 4, lax.rem(ch // 2, 2), lax.rem(ch, 2)
    other = 1 - c

    def chip(dz, dy):
        return lax.rem(z + dz + 4, 4) * 2 + (yh if dy == 0 else 1 - yh)

    up = (ctx, chip(1, 0) * 2 + c)
    down = (ctx, chip(-1, 0) * 2 + c)
    over = (ctx, chip(0, 1) * 2 + c)
    sib = (ctx, chip(0, 0) * 2 + other)

    def ring(k):
        return lax.rem(ctx + k, CTX)

    index = {}
    started = {}

    def slot(name):
        if name not in index:
            index[name] = len(index)
        return index[name]

    def send(name, src, dst, to):
        i = slot(name)
        cp = pltpu.make_async_remote_copy(
            src_ref=src, dst_ref=dst, send_sem=ss.at[i], recv_sem=rs.at[i],
            device_id=to, device_id_type=MESH,
        )
        cp.start()
        started[name] = cp

    def arrived(name, region):
        i = slot(name)
        pltpu.make_async_remote_copy(
            src_ref=region, dst_ref=region, send_sem=ss.at[i], recv_sem=rs.at[i],
            device_id=sib, device_id_type=MESH,
        ).wait_recv()

    def drain(prefix):
        for name in [n for n in started if n.startswith(prefix)]:
            started.pop(name).wait_send()

    local = []

    def fetch(src, dst):
        cp = pltpu.make_async_copy(src, dst, ls.at[len(local)])
        local.append(cp)
        cp.start()
        return cp

    barrier = pltpu.get_barrier_semaphore()
    partners = [up, down, over, sib] + [(ring(k), ch) for k in range(1, CTX)]
    for p in partners:
        pl.semaphore_signal(barrier, inc=1, device_id=p, device_id_type=MESH)
    mine = chip(0, 0)
    tok_in = fetch(tok_hbm, G.at[mine * 2 + c])
    filt_in = fetch(filt_hbm, TF)
    order = [(0, 0), (1, 0), (-1, 0), (0, 1), (2, 0), (1, 1), (-1, 1), (2, 1)]
    w_in = {}
    for d in order:
        r = pl.ds(pl.multiple_of(chip(*d) * 1024, 1024), 1024)
        w_in[d] = (fetch(wv_hbm.at[r], WV.at[r]), fetch(wg_hbm.at[r], WG.at[r]))
    fwd_in = fetch(fwd_hbm, FWD)
    inv_in = fetch(inv_hbm, INV)
    tok_in.wait()
    pl.semaphore_wait(barrier, len(partners))

    def piece(d, part, core=None):
        return G.at[chip(*d) * 2 + (c if core is None else core), rows_of(part)]

    def gsend(name, d, part, to):
        send("g_" + name, piece(d, part), piece(d, part), to)

    def gwait(name, d, part):
        arrived("g_" + name, piece(d, part))

    sibs = {}

    def to_sib(d, *parts):
        for part in parts:
            n = len(sibs)
            sibs[n] = (d, part)
            gsend("s%d" % n, d, part, sib)

    def from_sib(d):
        for n in [n for n in sibs if sibs[n][0] == d]:
            arrived("g_s%d" % n, piece(d, sibs.pop(n)[1], other))
            sibs[n] = (None, None)

    gsend("pa", (0, 0), A, up)
    gsend("ma", (0, 0), A, down)
    gsend("y1", (0, 0), B, over)
    gsend("pb", (0, 0), B, up)
    gsend("mb", (0, 0), B, down)
    gsend("y2", (0, 0), A, over)
    to_sib((0, 0), ALL)

    def pack_into(dst, p, top, bot):
        lo = low_lanes(HALF)
        dst[2 * p] = jnp.where(lo, top, swap(bot)).astype(BF16)
        dst[2 * p + 1] = jnp.where(lo, swap(top), bot).astype(BF16)

    filt_in.wait()

    def filt_pack(p, carry):
        block = TF[pl.ds(pl.multiple_of(p * 128, 128), 128), :].astype(F32).T
        pack_into(HSND, p, block[:HALF], block[HALF:])
        return carry

    lax.fori_loop(0, 4, filt_pack, 0)
    for k in (4, 3, 5, 2, 6, 1, 7):
        send("h_%d" % k, HSND.at[ring(k)], HR.at[ctx], (ring(k), ch))
    HR[ctx] = HSND[ctx]

    def project(acc, w, d, first=False):
        q = chip(*d)

        def body(n, carry):
            cols = pl.ds(pl.multiple_of(n * 256, 256), 256)
            r0 = pl.ds(pl.multiple_of(q * 1024, 1024), 512)
            r1 = pl.ds(pl.multiple_of(q * 1024 + 512, 512), 512)
            total = dot(G[2 * q], w[r0, cols]) + dot(G[2 * q + 1], w[r1, cols])
            acc[:, cols] = total if first else acc[:, cols] + total
            return carry

        lax.fori_loop(0, 2, body, 0)

    def both(d, first=False):
        from_sib(d)
        w_in[d][0].wait()
        w_in[d][1].wait()
        project(acc_v, WV, d, first)
        project(acc_g, WG, d, first)

    both((0, 0), True)
    gwait("pa", (-1, 0), A)
    gsend("p5", (-1, 0), A0, up)
    gsend("y3", (-1, 0), A, over)
    gwait("ma", (1, 0), A)
    gsend("m5", (1, 0), A1, down)
    gsend("y4", (1, 0), A, over)
    to_sib((-1, 0), A)
    to_sib((1, 0), A)
    gwait("y1", (0, 1), B)
    gsend("p7", (0, 1), B0, up)
    gsend("m7", (0, 1), B1, down)
    gsend("p8", (0, 1), B1, up)
    gsend("m8", (0, 1), B0, down)
    to_sib((0, 1), B)
    gwait("pb", (-1, 0), B)
    gsend("p6", (-1, 0), B0, up)
    gwait("mb", (1, 0), B)
    gsend("m6", (1, 0), B1, down)
    to_sib((-1, 0), B)
    to_sib((1, 0), B)
    gwait("y2", (0, 1), A)
    to_sib((0, 1), A)
    both((1, 0))
    gwait("p5", (2, 0), A0)
    gsend("y5", (2, 0), A0, over)
    gwait("m5", (2, 0), A1)
    gsend("y6", (2, 0), A1, over)
    to_sib((2, 0), A0, A1)
    both((-1, 0))
    gwait("p7", (-1, 1), B0)
    gsend("p9", (-1, 1), B0, up)
    gwait("m7", (1, 1), B1)
    gsend("m9", (1, 1), B1, down)
    to_sib((-1, 1), B0)
    to_sib((1, 1), B1)

    def out_cols(q, core):
        return pl.ds(pl.multiple_of((2 * q + core) * N, N), N)

    wo_in = []
    for q in range(CHIPS):
        wo_in.append(fetch(wo_hbm.at[:, out_cols(q, c)], WO.at[q, pl.ds(0, N)]))
        send("w_%d" % q, wo_hbm.at[:, out_cols(q, other)], WO.at[q, pl.ds(N, N)], sib)

    both((0, 1))
    gwait("y3", (-1, 1), A)
    to_sib((-1, 1), A)
    gwait("p8", (-1, 1), B1)
    gwait("m8", (1, 1), B0)
    to_sib((-1, 1), B1)
    to_sib((1, 1), B0)
    gwait("p6", (2, 0), B0)
    gwait("m6", (2, 0), B1)
    to_sib((2, 0), B0, B1)
    gwait("y4", (1, 1), A)
    to_sib((1, 1), A)
    both((2, 0))
    both((-1, 1))
    both((1, 1))
    last = (2, 1)
    gwait("y5", last, A0)
    to_sib(last, A0)
    gwait("y6", last, A1)
    to_sib(last, A1)
    gwait("p9", last, B0)
    to_sib(last, B0)
    gwait("m9", last, B1)
    to_sib(last, B1)
    from_sib(last)
    w_in[last][0].wait()
    w_in[last][1].wait()
    project(acc_v, WV, last)

    for p in range(4):
        cols = slice(128 * p, 128 * p + 128)
        pack_into(VS, p, acc_v[:HALF, cols], acc_v[HALF:, cols])
    for k in (4, 3, 5, 2, 6, 1, 7):
        send("v_%d" % k, VS.at[ring(k)], XR.at[ctx], (ring(k), ch))
    XR[ctx] = VS[ctx]
    project(acc_g, WG, last)

    fwd_in.wait()
    inv_in.wait()
    for k in range(1, CTX):
        arrived("h_%d" % k, HR.at[ring(CTX - k)])

    def spread_filter(i, carry):
        lo = low_lanes(HALF)
        h = HR[i].astype(F32)
        s = swap(h)
        HQ[pl.ds(pl.multiple_of(i * N, N), HALF), :] = jnp.where(lo, h, s).astype(BF16)
        HQ[pl.ds(pl.multiple_of(i * N + HALF, HALF), HALF), :] = jnp.where(lo, s, h).astype(BF16)
        return carry

    lax.fori_loop(0, CTX, spread_filter, 0)

    def filter_spectra(j, carry):
        b0 = HQ[pl.ds(pl.multiple_of(j * N, N), HALF), :]
        b1 = HQ[pl.ds(pl.multiple_of(j * N + HALF, HALF), HALF), :]
        s = dot(FWD[:, :HALF], jnp.concatenate([b0, b1], axis=1))
        HS[2 * j] = s[:, :128]
        HS[2 * j + 1] = s[:, 128:]
        return carry

    lax.fori_loop(0, 8, filter_spectra, 0)

    for k in range(1, CTX):
        arrived("v_%d" % k, XR.at[ring(CTX - k)])
    XQ[pl.ds(0, HALF), :] = jnp.zeros((HALF, 128), BF16)
    lo = low_lanes(HALF)
    XQ[pl.ds(HALF, HALF), :] = jnp.where(lo, 0.0, swap(XR[0].astype(F32))).astype(BF16)
    XQ[pl.ds(N, HALF), :] = XR[0]

    def spread_values(i, carry):
        lo = low_lanes(HALF)
        now = XR[i]
        x = jnp.where(lo, now.astype(F32), XR[i - 1].astype(F32))
        XQ[pl.ds(pl.multiple_of(i * N + HALF, HALF), HALF), :] = swap(x).astype(BF16)
        XQ[pl.ds(pl.multiple_of(i * N + N, N), HALF), :] = now
        return carry

    lax.fori_loop(1, CTX, spread_values, 0)

    def value_spectra(j, carry):
        b0 = XQ[pl.ds(pl.multiple_of(j * N, N), N), :]
        b1 = XQ[pl.ds(pl.multiple_of(j * N + HALF, HALF), N), :]
        s = dot(FWD[...], jnp.concatenate([b0, b1], axis=1))
        XS[2 * j] = s[:, :128]
        XS[2 * j + 1] = s[:, 128:]
        return carry

    lax.fori_loop(0, 8, value_spectra, 0)

    def multiply(t, carry):
        re = pl.ds(pl.multiple_of(t * 8, 8), 8)
        im = pl.ds(pl.multiple_of(t * 8 + HALF, 8), 8)
        xr = [XS[s, re, :] for s in range(16)]
        xi = [XS[s, im, :] for s in range(16)]
        yr, yi = [None] * 8, [None] * 8
        for d in range(16):
            hr, hi = HS[d, re, :], HS[d, im, :]
            for i in range(8):
                s = 2 * i - d + 1
                if s < 0:
                    continue
                r = hr * xr[s] - hi * xi[s]
                m = hr * xi[s] + hi * xr[s]
                yr[i] = r if yr[i] is None else yr[i] + r
                yi[i] = m if yi[i] is None else yi[i] + m
        for i in range(8):
            YP[i, re, :] = yr[i]
            YP[i, im, :] = yi[i]
        return carry

    lax.fori_loop(0, HALF // 8, multiply, 0)

    def back(j, carry):
        s = jnp.concatenate([YP[2 * j].astype(BF16), YP[2 * j + 1].astype(BF16)], axis=1)
        y = dot(INV[...], s).astype(BF16)
        YS[2 * j] = y[:, :128]
        YS[2 * j + 1] = y[:, 128:]
        return carry

    lax.fori_loop(0, 4, back, 0)
    for k in (4, 3, 5, 2, 6, 1, 7):
        send("y_%d" % k, YS.at[ring(k)], YR.at[ctx], (ring(k), ch))
    YR[ctx] = YS[ctx]
    drain("g_")
    for k in range(1, CTX):
        arrived("y_%d" % k, YR.at[ring(CTX - k)])

    for p in range(4):
        cols = slice(128 * p, 128 * p + 128)
        r0, r1 = YR[2 * p].astype(F32), YR[2 * p + 1].astype(F32)
        gate = acc_g[:, cols].astype(BF16).astype(F32)
        GA[:HALF, cols] = (jnp.where(lo, r0, swap(r1)) * gate[:HALF]).astype(BF16)
        GA[HALF:, cols] = (jnp.where(lo, swap(r0), r1) * gate[HALF:]).astype(BF16)
    send("a_0", GA, GB, sib)
    for cp in wo_in:
        cp.wait()
    for q in range(CHIPS):
        arrived("w_%d" % q, WO.at[q, pl.ds(N, N)])
    arrived("a_0", GB)

    def mix(*ds):
        for d in ds:
            q = chip(*d)

            def body(n, carry):
                cols = pl.ds(pl.multiple_of(n * 256, 256), 256)
                total = dot(GA[...], WO[q, :N, cols]) + dot(GB[...], WO[q, N:, cols])
                G[q, :, cols] = total.astype(BF16)
                return carry

            lax.fori_loop(0, 2, body, 0)

    def sums(d, part):
        return G.at[chip(*d), rows_of(part)]

    def rsend(name, d, part, buf, to):
        send("r_" + name, sums(d, part), buf, to)

    def radd(name, buf, d, part):
        arrived("r_" + name, buf)
        ref = sums(d, part)
        ref[...] = (ref[...].astype(F32) + buf[...].astype(F32)).astype(BF16)

    nb, n0, n1, na = B[1], A0[1], A1[1], A[1]
    def cut(ref, start, size):
        return ref.at[pl.ds(start, size)]

    off, pos = {}, 0
    for name, size in (
        ("z2y", 144), ("z2o", 144), ("z1y0", 144), ("z1y1", 144), ("z1o0", 144), ("z1o1", 144),
        ("a2", 112), ("a1x", 112), ("a1y", 112),
    ):
        off[name] = (pos, size)
        pos += size

    def rp(name):
        return cut(RP, *off[name])

    def rm(name):
        return cut(RM, *off[name])

    mix((2, 1))
    rsend("ya0", (2, 1), A, RYA.at[0], over)
    rsend("p_z2y", (2, 1), B0, rp("z2y"), up)
    rsend("m_z2y", (2, 1), B1, rm("z2y"), down)
    mix((2, 0))
    rsend("p_z2o", (2, 0), B0, rp("z2o"), up)
    rsend("m_z2o", (2, 0), B1, rm("z2o"), down)
    mix((1, 1), (-1, 1))
    rsend("ya1", (1, 1), A, RYA.at[1], over)
    rsend("ya2", (-1, 1), A, RYA.at[2], over)
    rsend("p_z1y1", (1, 1), B1, rp("z1y1"), up)
    rsend("m_z1y1", (-1, 1), B0, rm("z1y1"), down)
    mix((0, 1))
    rsend("ya3", (0, 1), A, RYA.at[3], over)
    mix((1, 0), (-1, 0))
    rsend("p_z1o1", (1, 0), B1, rp("z1o1"), up)
    rsend("m_z1o1", (-1, 0), B0, rm("z1o1"), down)
    radd("p_z2y", rp("z2y"), (1, 1), B0)
    rsend("p_z1y0", (1, 1), B0, rp("z1y0"), up)
    radd("m_z2y", rm("z2y"), (-1, 1), B1)
    rsend("m_z1y0", (-1, 1), B1, rm("z1y0"), down)
    radd("ya0", RYA.at[0], (2, 0), A)
    rsend("p_a2", (2, 0), A0, rp("a2"), up)
    rsend("m_a2", (2, 0), A1, rm("a2"), down)
    mix((0, 0))
    radd("p_z2o", rp("z2o"), (1, 0), B0)
    rsend("p_z1o0", (1, 0), B0, rp("z1o0"), up)
    radd("m_z2o", rm("z2o"), (-1, 0), B1)
    rsend("m_z1o0", (-1, 0), B1, rm("z1o0"), down)
    radd("p_z1y1", rp("z1y1"), (0, 1), B1)
    radd("m_z1y1", rm("z1y1"), (0, 1), B0)
    radd("ya1", RYA.at[1], (1, 0), A)
    rsend("p_a1x", (1, 0), A1, rp("a1x"), up)
    radd("p_z1y0", rp("z1y0"), (0, 1), B0)
    radd("m_z1y0", rm("z1y0"), (0, 1), B1)
    rsend("yb", (0, 1), B, RYB, over)
    radd("ya2", RYA.at[2], (-1, 0), A)
    rsend("m_a1x", (-1, 0), A0, rm("a1x"), down)
    radd("p_a2", rp("a2"), (1, 0), A0)
    rsend("p_a1y", (1, 0), A0, rp("a1y"), up)
    radd("m_a2", rm("a2"), (-1, 0), A1)
    rsend("m_a1y", (-1, 0), A1, rm("a1y"), down)

    def total(part, *bufs):
        value = sums((0, 0), part)[...].astype(F32)
        for b in bufs:
            value = value + b[...].astype(F32)
        out_ref[rows_of(part), :] = value.astype(BF16)

    arrived("r_ya3", RYA.at[3])
    for name in ("z1o1", "z1o0"):
        arrived("r_p_" + name, rp(name))
        arrived("r_m_" + name, rm(name))
    arrived("r_yb", RYB)
    total(B0, rp("z1o0"), rm("z1o1"), cut(RYB, 0, 144))
    total(B1, rp("z1o1"), rm("z1o0"), cut(RYB, 144, 144))
    for name in ("a1x", "a1y"):
        arrived("r_p_" + name, rp(name))
        arrived("r_m_" + name, rm(name))
    total(A0, cut(RYA.at[3], 0, 112), rp("a1y"), rm("a1x"))
    total(A1, cut(RYA.at[3], 112, 112), rp("a1x"), rm("a1y"))
    drain("")


def on_device(tokens, proj_value, proj_gate, conv_filter, proj_output):
    forward, inverse = tables()
    anywhere = pl.BlockSpec(memory_space=pl.ANY)
    vm = pltpu.VMEM
    return pl.pallas_call(
        kernel,
        out_shape=jax.ShapeDtypeStruct((N, N), BF16),
        in_specs=[anywhere] * 7,
        out_specs=pl.BlockSpec(memory_space=pltpu.VMEM),
        scratch_shapes=[
            vm((16, N, N), BF16),
            vm((8192, N), BF16),
            vm((8192, N), BF16),
            vm((CHIPS, 2 * N, N), BF16),
            vm((2 * HALF, 2 * HALF), BF16),
            vm((HALF, 2 * HALF), BF16),
            vm((N, N), BF16),
            vm((N, N), F32),
            vm((N, N), F32),
            vm((CTX, HALF, 128), BF16),
            vm((CTX, HALF, 128), BF16),
            vm((CTX, HALF, 128), BF16),
            vm((CTX, HALF, 128), BF16),
            vm((CTX, HALF, 128), BF16),
            vm((CTX, HALF, 128), BF16),
            vm((17 * HALF, 128), BF16),
            vm((16 * HALF, 128), BF16),
            vm((16, N, 128), F32),
            vm((16, N, 128), F32),
            vm((8, N, 128), F32),
            vm((N, N), BF16),
            vm((N, N), BF16),
            vm((4, A[1], N), BF16),
            vm((B[1], N), BF16),
            vm((1200, N), BF16),
            vm((1200, N), BF16),
            pltpu.SemaphoreType.DMA((TRANSFERS,)),
            pltpu.SemaphoreType.DMA((TRANSFERS,)),
            pltpu.SemaphoreType.DMA((40,)),
        ],
        compiler_params=pltpu.CompilerParams(
            collective_id=0, has_side_effects=True, vmem_limit_bytes=60 * 2**20
        ),
        name="hyena_block",
    )(
        tokens, proj_value, proj_gate, conv_filter, proj_output,
        jnp.asarray(forward), jnp.asarray(inverse),
    )


def solution(mesh):
    in_specs = (P("ctx", "ch"), P(None, "ch"), P(None, "ch"), P("ch", "ctx"), P("ch", None))
    return jax.shard_map(
        on_device, mesh=mesh, in_specs=in_specs, out_specs=P("ctx", "ch"), check_vma=False
    )
```

time: 268 us -> 108 us (0.40)
  waiting for transfers between devices: 175 us -> 0 us
  Pallas kernels: 0 us -> 106 us
  matrix products: 54 us -> 0 us
  between operations: 13.7 us -> 0.01 us
  blocking collectives: 11.2 us -> 0 us
  starting transfers between devices: 10.1 us -> 0 us
    pallas_call x0 -> x1, Pallas kernels: none -> 106 us  [on_device(): pl.pallas_call(kernel, out_shape=jax.ShapeDtypeStruct((N, N), BF16), in_s...]
    reduce_scatter x1 -> x0, waiting for transfers between devices: 100 us -> none  [on_device(): lax.psum_scatter(partial_terms.astype(jnp.bfloat16), 'ch', scatter_dimens...]
    all_gather x1 -> x0, waiting for transfers between devices: 62.5 us -> none  [on_device(): segment = lax.all_gather(tokens, 'ch', axis=1, tiled=True)]
    dot_general x21 -> x0, matrix products: 54 us -> none  [the longest x1 11.1 us: on_device(): lax.dot_general(proj_value, segment, contract, preferred_element_type=jnp...]
    all_to_all x2 -> x0, waiting for transfers between devices: 11.4 us -> none  [the longest x1 8.26 us: on_device(): lax.all_to_all(conv_filter, 'ctx', split_axis=0, concat_axis=1, tiled=True)]
    all_to_all x1 -> x0, blocking collectives: 11.2 us -> none  [on_device(): lax.all_to_all(result_major.astype(jnp.bfloat16), 'ctx', split_axis=1, co...]
    all_to_all x2 -> x0, starting transfers between devices: 9.87 us -> none  [the longest x1 5.87 us: on_device(): lax.all_to_all(conv_filter, 'ctx', split_axis=0, concat_axis=1, tiled=True)]
  transfers between devices with their start and end apart: 4 -> 0, of which waited for: 4 -> 0; matrix products, arithmetic and copies ran while one was open for 5% -> 0% of each run, Pallas kernels for 0% -> 0%
where the time goes in v1:
time: 108 us
  Pallas kernels  106 us (98%)
  local copies, waits for them, and re-layouts  1.87 us (2%)
    pallas_call x1, Pallas kernels, on_device(): pl.pallas_call(kernel, out_shape=jax.ShapeDtypeStruct((N, N), BF16), in_s...  106 us

profile of v1, /device:TPU:1, one launch (start us, length us, event | category | flops | bytes accessed | tf_op | source)
XLA Modules:
  0.0 107.8 jit_solution(12404936227670232948)
XLA Ops:
  0.0 105.9 %hyena_block.1 = bf16[512,512]{1,0:T(8,128)(2,1)} custom-call(bf16[512,512]{1,0:T(8,128)(2,1)} %tok_hbm.1, bf16[8192,512]{1,0:T(8,128)(2,1)} %wv_hbm.1, bf16[8192,512]{1,0:T(8,128)(2,1)} %wg_hbm.1, bf16[512,512]{1,0:T(8,128)(2,1)} %filt_hbm.1, bf16[512,8192]{1,0:T(8,128)(2,1)} %wo_hbm.1, bf16[512,512]{1,0:T(8,128)(2,1)} %constant.4.clone.fwd_hbm, ...), custom_call_target="tpu_custom_call" | custom-call | tf_op jit(solution)/shard_map/hyena_block/pallas_call | solution.py:490
  105.9 1.9 %copy.9 = bf16[512,512]{1,0:T(8,128)(2,1)} copy(bf16[512,512]{1,0:T(8,128)(2,1)} %hyena_block.1) | data formatting | bytes 1048576

commit v2 on v1

--- a/solution.py
+++ b/solution.py
@@ -24,16 +24,17 @@
     (224, 288),
     (0, 512),
 )
+GA0, GA1, GA_, GB0, GB1, GB_ = ((0, 80), (80, 80), (0, 160), (160, 176), (336, 176), (160, 352))
 TRANSFERS = 128
 
 
 def tables():
-    k = np.arange(HALF)[:, None]
+    k = np.concatenate([np.arange(0, HALF, 2), np.arange(1, HALF, 2)])[:, None]
     n = np.arange(2 * HALF)[None, :]
     angle = math.pi / (2 * HALF) * ((2 * k + 1) * n % (4 * HALF))
     forward = np.concatenate([np.cos(angle), -np.sin(angle)], axis=0)
     inverse = forward[:, HALF:].T * (1.0 / HALF)
-    return forward.astype(jnp.bfloat16), inverse.astype(jnp.bfloat16)
+    return forward[:, :HALF].astype(jnp.bfloat16), inverse.astype(jnp.bfloat16)
 
 
 def dot(a, b):
@@ -55,7 +56,7 @@
 def kernel(
     tok_hbm, wv_hbm, wg_hbm, filt_hbm, wo_hbm, fwd_hbm, inv_hbm, out_ref,
     G, WV, WG, WO, FWD, INV, TF, acc_v, acc_g, VS, HSND, XR, HR, YS, YR,
-    XQ, HQ, XS, HS, YP, GA, GB, RYA, RYB, RP, RM, ss, rs, ls,
+    HQ, XS, HS, YP, GA, GB, RYA, RYB, RP, RM, ss, rs, ls,
 ):
     ctx = lax.axis_index("ctx")
     ch = lax.axis_index("ch")
@@ -117,44 +118,52 @@
     tok_in = fetch(tok_hbm, G.at[mine * 2 + c])
     filt_in = fetch(filt_hbm, TF)
     order = [(0, 0), (1, 0), (-1, 0), (0, 1), (2, 0), (1, 1), (-1, 1), (2, 1)]
+    tok_in.wait()
+    pl.semaphore_wait(barrier, len(partners))
+
+    def piece(d, part, core=None):
+        return G.at[chip(*d) * 2 + (c if core is None else core), rows_of(part)]
+
+    def gsend(name, d, part, to):
+        send("g_" + name, piece(d, part), piece(d, part), to)
+
+    def gwait(name, d, part):
+        arrived("g_" + name, piece(d, part))
+
+    sibs = {}
+
+    def to_sib(d, *parts):
+        for part in parts:
+            n = len(sibs)
+            sibs[n] = (d, part)
+            gsend("s%d" % n, d, part, sib)
+
+    def from_sib(d):
+        for n in [n for n in sibs if sibs[n][0] == d]:
+            arrived("g_s%d" % n, piece(d, sibs.pop(n)[1], other))
+            sibs[n] = (None, None)
+
+    gsend("pa", (0, 0), GA_, up)
+    gsend("ma", (0, 0), GA_, down)
+    gsend("y1", (0, 0), GB_, over)
+    gsend("pb", (0, 0), GB_, up)
+    gsend("mb", (0, 0), GB_, down)
+    gsend("y2", (0, 0), GA_, over)
+    to_sib((0, 0), ALL)
     w_in = {}
     for d in order:
         r = pl.ds(pl.multiple_of(chip(*d) * 1024, 1024), 1024)
         w_in[d] = (fetch(wv_hbm.at[r], WV.at[r]), fetch(wg_hbm.at[r], WG.at[r]))
     fwd_in = fetch(fwd_hbm, FWD)
     inv_in = fetch(inv_hbm, INV)
-    tok_in.wait()
-    pl.semaphore_wait(barrier, len(partners))
-
-    def piece(d, part, core=None):
-        return G.at[chip(*d) * 2 + (c if core is None else core), rows_of(part)]
-
-    def gsend(name, d, part, to):
-        send("g_" + name, piece(d, part), piece(d, part), to)
-
-    def gwait(name, d, part):
-        arrived("g_" + name, piece(d, part))
-
-    sibs = {}
-
-    def to_sib(d, *parts):
-        for part in parts:
-            n = len(sibs)
-            sibs[n] = (d, part)
-            gsend("s%d" % n, d, part, sib)
-
-    def from_sib(d):
-        for n in [n for n in sibs if sibs[n][0] == d]:
-            arrived("g_s%d" % n, piece(d, sibs.pop(n)[1], other))
-            sibs[n] = (None, None)
-
-    gsend("pa", (0, 0), A, up)
-    gsend("ma", (0, 0), A, down)
-    gsend("y1", (0, 0), B, over)
-    gsend("pb", (0, 0), B, up)
-    gsend("mb", (0, 0), B, down)
-    gsend("y2", (0, 0), A, over)
-    to_sib((0, 0), ALL)
+
+    def out_cols(q, core):
+        return pl.ds(pl.multiple_of((2 * q + core) * N, N), N)
+
+    wo_in = []
+    for q in range(CHIPS):
+        send("w_%d" % q, wo_hbm.at[:, out_cols(q, other)], WO.at[q, pl.ds(N, N)], sib)
+        wo_in.append(fetch(wo_hbm.at[:, out_cols(q, c)], WO.at[q, pl.ds(0, N)]))
 
     def pack_into(dst, p, top, bot):
         lo = low_lanes(HALF)
@@ -169,103 +178,107 @@
         return carry
 
     lax.fori_loop(0, 4, filt_pack, 0)
-    for k in (4, 3, 5, 2, 6, 1, 7):
-        send("h_%d" % k, HSND.at[ring(k)], HR.at[ctx], (ring(k), ch))
+
+    def send_filter(*ks):
+        for k in ks:
+            send("h_%d" % k, HSND.at[ring(k)], HR.at[ctx], (ring(k), ch))
+
+    send_filter(4, 2, 6)
     HR[ctx] = HSND[ctx]
 
-    def project(acc, w, d, first=False):
-        q = chip(*d)
-
+    def project(acc, w, d, first=False, cores=(0, 1)):
         def body(n, carry):
             cols = pl.ds(pl.multiple_of(n * 256, 256), 256)
-            r0 = pl.ds(pl.multiple_of(q * 1024, 1024), 512)
-            r1 = pl.ds(pl.multiple_of(q * 1024 + 512, 512), 512)
-            total = dot(G[2 * q], w[r0, cols]) + dot(G[2 * q + 1], w[r1, cols])
+            total = None
+            for core in cores:
+                g = chip(*d) * 2 + core
+                r = pl.ds(pl.multiple_of(g * N, N), N)
+                term = dot(G[g], w[r, cols])
+                total = term if total is None else total + term
             acc[:, cols] = total if first else acc[:, cols] + total
             return carry
 
         lax.fori_loop(0, 2, body, 0)
 
-    def both(d, first=False):
+    def ready(d):
         from_sib(d)
         w_in[d][0].wait()
         w_in[d][1].wait()
+
+    def both(d, first=False):
+        ready(d)
         project(acc_v, WV, d, first)
         project(acc_g, WG, d, first)
 
     both((0, 0), True)
-    gwait("pa", (-1, 0), A)
-    gsend("p5", (-1, 0), A0, up)
-    gsend("y3", (-1, 0), A, over)
-    gwait("ma", (1, 0), A)
-    gsend("m5", (1, 0), A1, down)
-    gsend("y4", (1, 0), A, over)
-    to_sib((-1, 0), A)
-    to_sib((1, 0), A)
-    gwait("y1", (0, 1), B)
-    gsend("p7", (0, 1), B0, up)
-    gsend("m7", (0, 1), B1, down)
-    gsend("p8", (0, 1), B1, up)
-    gsend("m8", (0, 1), B0, down)
-    to_sib((0, 1), B)
-    gwait("pb", (-1, 0), B)
-    gsend("p6", (-1, 0), B0, up)
-    gwait("mb", (1, 0), B)
-    gsend("m6", (1, 0), B1, down)
-    to_sib((-1, 0), B)
-    to_sib((1, 0), B)
-    gwait("y2", (0, 1), A)
-    to_sib((0, 1), A)
+    gwait("pa", (-1, 0), GA_)
+    gsend("p5", (-1, 0), GA0, up)
+    gsend("y3", (-1, 0), GA_, over)
+    gwait("ma", (1, 0), GA_)
+    gsend("m5", (1, 0), GA1, down)
+    gsend("y4", (1, 0), GA_, over)
+    to_sib((-1, 0), GA_)
+    to_sib((1, 0), GA_)
+    gwait("y1", (0, 1), GB_)
+    gsend("p7", (0, 1), GB0, up)
+    gsend("m7", (0, 1), GB1, down)
+    to_sib((0, 1), GB_)
+    gwait("pb", (-1, 0), GB_)
+    gsend("p6", (-1, 0), GB0, up)
+    gsend("p8", (0, 1), GB1, up)
+    gwait("mb", (1, 0), GB_)
+    gsend("m6", (1, 0), GB1, down)
+    gsend("m8", (0, 1), GB0, down)
+    to_sib((1, 0), GB_)
+    to_sib((-1, 0), GB_)
+    gwait("y2", (0, 1), GA_)
+    to_sib((0, 1), GA_)
+    send_filter(3, 5, 1, 7)
+    gwait("p5", (2, 0), GA0)
+    gsend("y5", (2, 0), GA0, over)
+    gwait("m5", (2, 0), GA1)
+    gsend("y6", (2, 0), GA1, over)
+    to_sib((2, 0), GA0, GA1)
     both((1, 0))
-    gwait("p5", (2, 0), A0)
-    gsend("y5", (2, 0), A0, over)
-    gwait("m5", (2, 0), A1)
-    gsend("y6", (2, 0), A1, over)
-    to_sib((2, 0), A0, A1)
     both((-1, 0))
-    gwait("p7", (-1, 1), B0)
-    gsend("p9", (-1, 1), B0, up)
-    gwait("m7", (1, 1), B1)
-    gsend("m9", (1, 1), B1, down)
-    to_sib((-1, 1), B0)
-    to_sib((1, 1), B1)
-
-    def out_cols(q, core):
-        return pl.ds(pl.multiple_of((2 * q + core) * N, N), N)
-
-    wo_in = []
-    for q in range(CHIPS):
-        wo_in.append(fetch(wo_hbm.at[:, out_cols(q, c)], WO.at[q, pl.ds(0, N)]))
-        send("w_%d" % q, wo_hbm.at[:, out_cols(q, other)], WO.at[q, pl.ds(N, N)], sib)
-
+    gwait("p7", (-1, 1), GB0)
+    gsend("p9", (-1, 1), GB0, up)
+    gwait("m7", (1, 1), GB1)
+    gsend("m9", (1, 1), GB1, down)
+    to_sib((-1, 1), GB0)
+    to_sib((1, 1), GB1)
     both((0, 1))
-    gwait("y3", (-1, 1), A)
-    to_sib((-1, 1), A)
-    gwait("p8", (-1, 1), B1)
-    gwait("m8", (1, 1), B0)
-    to_sib((-1, 1), B1)
-    to_sib((1, 1), B0)
-    gwait("p6", (2, 0), B0)
-    gwait("m6", (2, 0), B1)
-    to_sib((2, 0), B0, B1)
-    gwait("y4", (1, 1), A)
-    to_sib((1, 1), A)
+    gwait("y3", (-1, 1), GA_)
+    to_sib((-1, 1), GA_)
+    gwait("p6", (2, 0), GB0)
+    gwait("m6", (2, 0), GB1)
+    to_sib((2, 0), GB0, GB1)
     both((2, 0))
-    both((-1, 1))
-    both((1, 1))
+    gwait("y4", (1, 1), GA_)
+    to_sib((1, 1), GA_)
+    gwait("p8", (-1, 1), GB1)
+    gwait("m8", (1, 1), GB0)
+    to_sib((-1, 1), GB1)
+    to_sib((1, 1), GB0)
+    ready((-1, 1))
+    project(acc_v, WV, (-1, 1))
+    ready((1, 1))
+    project(acc_v, WV, (1, 1))
     last = (2, 1)
-    gwait("y5", last, A0)
-    to_sib(last, A0)
-    gwait("y6", last, A1)
-    to_sib(last, A1)
-    gwait("p9", last, B0)
-    to_sib(last, B0)
-    gwait("m9", last, B1)
-    to_sib(last, B1)
-    from_sib(last)
+    gwait("y5", last, GA0)
+    to_sib(last, GA0)
+    gwait("y6", last, GA1)
+    to_sib(last, GA1)
+    project(acc_g, WG, (-1, 1))
+    gwait("p9", last, GB0)
+    to_sib(last, GB0)
+    gwait("m9", last, GB1)
+    to_sib(last, GB1)
     w_in[last][0].wait()
     w_in[last][1].wait()
-    project(acc_v, WV, last)
+    project(acc_v, WV, last, cores=(c,))
+    from_sib(last)
+    project(acc_v, WV, last, cores=(other,))
 
     for p in range(4):
         cols = slice(128 * p, 128 * p + 128)
@@ -273,6 +286,7 @@
     for k in (4, 3, 5, 2, 6, 1, 7):
         send("v_%d" % k, VS.at[ring(k)], XR.at[ctx], (ring(k), ch))
     XR[ctx] = VS[ctx]
+    project(acc_g, WG, (1, 1))
     project(acc_g, WG, last)
 
     fwd_in.wait()
@@ -293,74 +307,72 @@
     def filter_spectra(j, carry):
         b0 = HQ[pl.ds(pl.multiple_of(j * N, N), HALF), :]
         b1 = HQ[pl.ds(pl.multiple_of(j * N + HALF, HALF), HALF), :]
-        s = dot(FWD[:, :HALF], jnp.concatenate([b0, b1], axis=1))
+        s = dot(FWD[...], jnp.concatenate([b0, b1], axis=1))
         HS[2 * j] = s[:, :128]
         HS[2 * j + 1] = s[:, 128:]
         return carry
 
     lax.fori_loop(0, 8, filter_spectra, 0)
 
-    for k in range(1, CTX):
-        arrived("v_%d" % k, XR.at[ring(CTX - k)])
-    XQ[pl.ds(0, HALF), :] = jnp.zeros((HALF, 128), BF16)
+    def value_spectrum(i):
+        XS[i] = dot(FWD[...], XR[i])
+
+    value_spectrum(ctx)
+
+    for k in (1, 7, 2, 6, 3, 5, 4):
+        i = ring(CTX - k)
+        arrived("v_%d" % k, XR.at[i])
+        value_spectrum(i)
+
     lo = low_lanes(HALF)
-    XQ[pl.ds(HALF, HALF), :] = jnp.where(lo, 0.0, swap(XR[0].astype(F32))).astype(BF16)
-    XQ[pl.ds(N, HALF), :] = XR[0]
-
-    def spread_values(i, carry):
-        lo = low_lanes(HALF)
-        now = XR[i]
-        x = jnp.where(lo, now.astype(F32), XR[i - 1].astype(F32))
-        XQ[pl.ds(pl.multiple_of(i * N + HALF, HALF), HALF), :] = swap(x).astype(BF16)
-        XQ[pl.ds(pl.multiple_of(i * N + N, N), HALF), :] = now
-        return carry
-
-    lax.fori_loop(1, CTX, spread_values, 0)
-
-    def value_spectra(j, carry):
-        b0 = XQ[pl.ds(pl.multiple_of(j * N, N), N), :]
-        b1 = XQ[pl.ds(pl.multiple_of(j * N + HALF, HALF), N), :]
-        s = dot(FWD[...], jnp.concatenate([b0, b1], axis=1))
-        XS[2 * j] = s[:, :128]
-        XS[2 * j + 1] = s[:, 128:]
-        return carry
-
-    lax.fori_loop(0, 8, value_spectra, 0)
-
-    def multiply(t, carry):
-        re = pl.ds(pl.multiple_of(t * 8, 8), 8)
-        im = pl.ds(pl.multiple_of(t * 8 + HALF, 8), 8)
-        xr = [XS[s, re, :] for s in range(16)]
-        xi = [XS[s, im, :] for s in range(16)]
-        yr, yi = [None] * 8, [None] * 8
-        for d in range(16):
-            hr, hi = HS[d, re, :], HS[d, im, :]
+
+    def multiply(even):
+        def body(t, carry):
+            re = pl.ds(pl.multiple_of(t * 8, 8), 8)
+            im = pl.ds(pl.multiple_of(t * 8 + HALF, 8), 8)
+            lo8 = low_lanes(8)
+            xr, xi = [], []
+            pr = pi = jnp.zeros((8, 128), F32)
             for i in range(8):
-                s = 2 * i - d + 1
-                if s < 0:
-                    continue
-                r = hr * xr[s] - hi * xi[s]
-                m = hr * xi[s] + hi * xr[s]
-                yr[i] = r if yr[i] is None else yr[i] + r
-                yi[i] = m if yi[i] is None else yi[i] + m
-        for i in range(8):
-            YP[i, re, :] = yr[i]
-            YP[i, im, :] = yi[i]
-        return carry
-
-    lax.fori_loop(0, HALF // 8, multiply, 0)
-
-    def back(j, carry):
-        s = jnp.concatenate([YP[2 * j].astype(BF16), YP[2 * j + 1].astype(BF16)], axis=1)
-        y = dot(INV[...], s).astype(BF16)
-        YS[2 * j] = y[:, :128]
-        YS[2 * j + 1] = y[:, 128:]
-        return carry
-
-    lax.fori_loop(0, 4, back, 0)
-    for k in (4, 3, 5, 2, 6, 1, 7):
-        send("y_%d" % k, YS.at[ring(k)], YR.at[ctx], (ring(k), ch))
-    YR[ctx] = YS[ctx]
+                ur, ui = XS[i, re, :], XS[i, im, :]
+                mr = swap(jnp.where(lo8, ur, pr))
+                mi = swap(jnp.where(lo8, ui, pi))
+                if even:
+                    xr += [pr + mi, mr + ui]
+                    xi += [pi - mr, mi - ur]
+                else:
+                    xr += [pr - mi, mr - ui]
+                    xi += [pi + mr, mi + ur]
+                pr, pi = ur, ui
+            yr, yi = [None] * 8, [None] * 8
+            for d in range(16):
+                hr, hi = HS[d, re, :], HS[d, im, :]
+                for i in range(8):
+                    s = 2 * i - d + 1
+                    if s < 0:
+                        continue
+                    r = hr * xr[s] - hi * xi[s]
+                    m = hr * xi[s] + hi * xr[s]
+                    yr[i] = r if yr[i] is None else yr[i] + r
+                    yi[i] = m if yi[i] is None else yi[i] + m
+            for i in range(8):
+                YP[i, re, :] = yr[i]
+                YP[i, im, :] = yi[i]
+            return carry
+
+        return body
+
+    lax.fori_loop(0, HALF // 16, multiply(True), 0)
+    lax.fori_loop(HALF // 16, HALF // 8, multiply(False), 0)
+
+    for k in (4, 3, 5, 2, 6, 1, 7, 0):
+        i = ring(k)
+        y = dot(INV[...], YP[i].astype(BF16)).astype(BF16)
+        if k:
+            YS[i] = y
+            send("y_%d" % k, YS.at[i], YR.at[ctx], (i, ch))
+        else:
+            YR[ctx] = y
     drain("g_")
     for k in range(1, CTX):
         arrived("y_%d" % k, YR.at[ring(CTX - k)])
@@ -371,12 +383,13 @@
         gate = acc_g[:, cols].astype(BF16).astype(F32)
         GA[:HALF, cols] = (jnp.where(lo, r0, swap(r1)) * gate[:HALF]).astype(BF16)
         GA[HALF:, cols] = (jnp.where(lo, swap(r0), r1) * gate[HALF:]).astype(BF16)
-    send("a_0", GA, GB, sib)
+        send("a_%d" % p, GA.at[:, cols], GB.at[:, cols], sib)
     for cp in wo_in:
         cp.wait()
     for q in range(CHIPS):
         arrived("w_%d" % q, WO.at[q, pl.ds(N, N)])
-    arrived("a_0", GB)
+    for p in range(4):
+        arrived("a_%d" % p, GB.at[:, 128 * p : 128 * p + 128])
 
     def mix(*ds):
         for d in ds:
@@ -489,7 +502,7 @@
     vm = pltpu.VMEM
     return pl.pallas_call(
         kernel,
-        out_shape=jax.ShapeDtypeStruct((N, N), BF16),
+        out_shape=pltpu.VMEM((N, N), BF16),
         in_specs=[anywhere] * 7,
         out_specs=pl.BlockSpec(memory_space=pltpu.VMEM),
         scratch_shapes=[
@@ -497,7 +510,7 @@
             vm((8192, N), BF16),
             vm((8192, N), BF16),
             vm((CHIPS, 2 * N, N), BF16),
-            vm((2 * HALF, 2 * HALF), BF16),
+            vm((2 * HALF, HALF), BF16),
             vm((HALF, 2 * HALF), BF16),
             vm((N, N), BF16),
             vm((N, N), F32),
@@ -508,9 +521,8 @@
             vm((CTX, HALF, 128), BF16),
             vm((CTX, HALF, 128), BF16),
             vm((CTX, HALF, 128), BF16),
-            vm((17 * HALF, 128), BF16),
             vm((16 * HALF, 128), BF16),
-            vm((16, N, 128), F32),
+            vm((8, N, 128), F32),
             vm((16, N, 128), F32),
             vm((8, N, 128), F32),
             vm((N, N), BF16),
@@ -524,7 +536,7 @@
             pltpu.SemaphoreType.DMA((40,)),
         ],
         compiler_params=pltpu.CompilerParams(
-            collective_id=0, has_side_effects=True, vmem_limit_bytes=60 * 2**20
+            collective_id=0, has_side_effects=True, vmem_limit_bytes=56 * 2**20
         ),
         name="hyena_block",
     )(

time: 108 us -> 101 us (0.935)
  Pallas kernels: 106 us -> 100 us
    pallas_call x1, Pallas kernels: 106 us -> 100 us  [on_device(): pl.pallas_call(kernel, out_shape=pltpu.VMEM((N, N), BF16), in_specs=[anyw...]
where the time goes in v2:
time: 101 us
  Pallas kernels  100 us (99%)
    pallas_call x1, Pallas kernels, on_device(): pl.pallas_call(kernel, out_shape=pltpu.VMEM((N, N), BF16), in_specs=[anyw...  100 us

profile of v2, /device:TPU:1, one launch (start us, length us, event | category | flops | bytes accessed | tf_op | source)
XLA Modules:
  0.0 101.1 jit_solution(15484929366856315541)
XLA Ops:
  0.0 100.2 %hyena_block.1 = bf16[512,512]{1,0:T(8,128)(2,1)S(1)} custom-call(bf16[512,512]{1,0:T(8,128)(2,1)} %tok_hbm.1, bf16[8192,512]{1,0:T(8,128)(2,1)} %wv_hbm.1, bf16[8192,512]{1,0:T(8,128)(2,1)} %wg_hbm.1, bf16[512,512]{1,0:T(8,128)(2,1)} %filt_hbm.1, bf16[512,8192]{1,0:T(8,128)(2,1)} %wo_hbm.1, bf16[512,256]{1,0:T(8,128)(2,1)} %constant.4.clone.fwd_hbm, ...), custom_call_target="tpu_custom_call" | custom-call | tf_op jit(solution)/shard_map/hyena_block/pallas_call | solution.py:503
  100.3 0.8 copy.9

commit v3 on v2

--- a/solution.py
+++ b/solution.py
@@ -15,17 +15,21 @@
 CTX = 8
 CHIPS = 8
 HALF = 256
-A0, A1, A, B0, B1, B, ALL = (
-    (0, 112),
-    (112, 112),
-    (0, 224),
-    (224, 144),
-    (368, 144),
-    (224, 288),
-    (0, 512),
-)
+ALL = (0, 512)
+QUARTER = 128
+
+
+def parts(base, *sizes):
+    a0, a1, b0, b1 = sizes
+    return (
+        (base, a0), (base + a0, a1), (base, a0 + a1),
+        (base + a0 + a1, b0), (base + a0 + a1 + b0, b1), (base + a0 + a1, b0 + b1),
+    )
+
+
+WAVES = (parts(0, 48, 48, 80, 80), parts(256, 48, 64, 80, 64))
 GA0, GA1, GA_, GB0, GB1, GB_ = ((0, 80), (80, 80), (0, 160), (160, 176), (336, 176), (160, 352))
-TRANSFERS = 128
+TRANSFERS = 192
 
 
 def tables():
@@ -365,134 +369,184 @@
     lax.fori_loop(0, HALF // 16, multiply(True), 0)
     lax.fori_loop(HALF // 16, HALF // 8, multiply(False), 0)
 
-    for k in (4, 3, 5, 2, 6, 1, 7, 0):
-        i = ring(k)
-        y = dot(INV[...], YP[i].astype(BF16)).astype(BF16)
-        if k:
-            YS[i] = y
-            send("y_%d" % k, YS.at[i], YR.at[ctx], (i, ch))
-        else:
-            YR[ctx] = y
+    for w in range(2):
+        for k in (4, 3, 5, 2, 6, 1, 7, 0):
+            i = ring(k)
+            y = dot(INV[pl.ds(QUARTER * w, QUARTER), :], YP[i].astype(BF16)).astype(BF16)
+            if k:
+                YS[w, i] = y
+                send("y%d_%d" % (w, k), YS.at[w, i], YR.at[w, ctx], (i, ch))
+            else:
+                YR[w, ctx] = y
+
+    def wave_rows(w):
+        return pl.ds(HALF * w, HALF)
+
+    def gate_wave(w):
+        for k in range(1, CTX):
+            arrived("y%d_%d" % (w, k), YR.at[w, ring(CTX - k)])
+        lo = low_lanes(QUARTER)
+        r = HALF * w
+        for p in range(4):
+            cols = slice(128 * p, 128 * p + 128)
+            r0, r1 = YR[w, 2 * p].astype(F32), YR[w, 2 * p + 1].astype(F32)
+            top = acc_g[QUARTER * w : QUARTER * w + QUARTER, cols].astype(BF16).astype(F32)
+            bot = acc_g[HALF + QUARTER * w : HALF + QUARTER * w + QUARTER, cols].astype(BF16).astype(F32)
+            GA[r : r + QUARTER, cols] = (jnp.where(lo, r0, swap(r1)) * top).astype(BF16)
+            GA[r + QUARTER : r + HALF, cols] = (jnp.where(lo, swap(r0), r1) * bot).astype(BF16)
+            send("a%d_%d" % (w, p), GA.at[wave_rows(w), cols], GB.at[wave_rows(w), cols], sib)
+
+    def gate_arrived(w):
+        for p in range(4):
+            arrived("a%d_%d" % (w, p), GB.at[wave_rows(w), 128 * p : 128 * p + 128])
+
+    gate_wave(0)
     drain("g_")
-    for k in range(1, CTX):
-        arrived("y_%d" % k, YR.at[ring(CTX - k)])
-
-    for p in range(4):
-        cols = slice(128 * p, 128 * p + 128)
-        r0, r1 = YR[2 * p].astype(F32), YR[2 * p + 1].astype(F32)
-        gate = acc_g[:, cols].astype(BF16).astype(F32)
-        GA[:HALF, cols] = (jnp.where(lo, r0, swap(r1)) * gate[:HALF]).astype(BF16)
-        GA[HALF:, cols] = (jnp.where(lo, swap(r0), r1) * gate[HALF:]).astype(BF16)
-        send("a_%d" % p, GA.at[:, cols], GB.at[:, cols], sib)
     for cp in wo_in:
         cp.wait()
     for q in range(CHIPS):
         arrived("w_%d" % q, WO.at[q, pl.ds(N, N)])
-    for p in range(4):
-        arrived("a_%d" % p, GB.at[:, 128 * p : 128 * p + 128])
-
-    def mix(*ds):
+    gate_arrived(0)
+
+    def mix(w, *ds):
+        rows = wave_rows(w)
         for d in ds:
             q = chip(*d)
 
             def body(n, carry):
                 cols = pl.ds(pl.multiple_of(n * 256, 256), 256)
-                total = dot(GA[...], WO[q, :N, cols]) + dot(GB[...], WO[q, N:, cols])
-                G[q, :, cols] = total.astype(BF16)
+                total = dot(GA[rows, :], WO[q, :N, cols]) + dot(GB[rows, :], WO[q, N:, cols])
+                G[q, rows, cols] = total.astype(BF16)
                 return carry
 
             lax.fori_loop(0, 2, body, 0)
+
+    def cut(ref, start, size):
+        return ref.at[pl.ds(start, size)]
+
+    place, room = {}, [0, 0]
+    for w in range(2):
+        A0, A1, A, B0, B1, B = WAVES[w]
+        for name, up_part, down_part in (
+            ("z2y", B0, B1), ("z2o", B0, B1), ("z1y0", B0, B1), ("z1y1", B1, B0), ("z1o0", B0, B1),
+            ("z1o1", B1, B0), ("a2", A0, A1), ("a1x", A1, A0), ("a1y", A0, A1),
+        ):
+            for side, part in ((0, up_part), (1, down_part)):
+                place["pm"[side] + name, w] = (room[side], part[1])
+                room[side] += part[1]
+
+    def inbox(name, w):
+        return cut(RP if name[0] == "p" else RM, *place[name, w])
+
+    def ya(k, w):
+        return RYA.at[w, k, pl.ds(0, WAVES[w][2][1])]
+
+    def yb(w):
+        return RYB.at[w, pl.ds(0, WAVES[w][5][1])]
 
     def sums(d, part):
         return G.at[chip(*d), rows_of(part)]
 
-    def rsend(name, d, part, buf, to):
-        send("r_" + name, sums(d, part), buf, to)
-
-    def radd(name, buf, d, part):
-        arrived("r_" + name, buf)
+    def pass_on(name, w, d, part):
+        send("r%d_%s" % (w, name), sums(d, part), inbox(name, w), up if name[0] == "p" else down)
+
+    def add(name, w, d, part, buf=None):
+        buf = inbox(name, w) if buf is None else buf
+        arrived("r%d_%s" % (w, name), buf)
         ref = sums(d, part)
         ref[...] = (ref[...].astype(F32) + buf[...].astype(F32)).astype(BF16)
 
-    nb, n0, n1, na = B[1], A0[1], A1[1], A[1]
-    def cut(ref, start, size):
-        return ref.at[pl.ds(start, size)]
-
-    off, pos = {}, 0
-    for name, size in (
-        ("z2y", 144), ("z2o", 144), ("z1y0", 144), ("z1y1", 144), ("z1o0", 144), ("z1o1", 144),
-        ("a2", 112), ("a1x", 112), ("a1y", 112),
-    ):
-        off[name] = (pos, size)
-        pos += size
-
-    def rp(name):
-        return cut(RP, *off[name])
-
-    def rm(name):
-        return cut(RM, *off[name])
-
-    mix((2, 1))
-    rsend("ya0", (2, 1), A, RYA.at[0], over)
-    rsend("p_z2y", (2, 1), B0, rp("z2y"), up)
-    rsend("m_z2y", (2, 1), B1, rm("z2y"), down)
-    mix((2, 0))
-    rsend("p_z2o", (2, 0), B0, rp("z2o"), up)
-    rsend("m_z2o", (2, 0), B1, rm("z2o"), down)
-    mix((1, 1), (-1, 1))
-    rsend("ya1", (1, 1), A, RYA.at[1], over)
-    rsend("ya2", (-1, 1), A, RYA.at[2], over)
-    rsend("p_z1y1", (1, 1), B1, rp("z1y1"), up)
-    rsend("m_z1y1", (-1, 1), B0, rm("z1y1"), down)
-    mix((0, 1))
-    rsend("ya3", (0, 1), A, RYA.at[3], over)
-    mix((1, 0), (-1, 0))
-    rsend("p_z1o1", (1, 0), B1, rp("z1o1"), up)
-    rsend("m_z1o1", (-1, 0), B0, rm("z1o1"), down)
-    radd("p_z2y", rp("z2y"), (1, 1), B0)
-    rsend("p_z1y0", (1, 1), B0, rp("z1y0"), up)
-    radd("m_z2y", rm("z2y"), (-1, 1), B1)
-    rsend("m_z1y0", (-1, 1), B1, rm("z1y0"), down)
-    radd("ya0", RYA.at[0], (2, 0), A)
-    rsend("p_a2", (2, 0), A0, rp("a2"), up)
-    rsend("m_a2", (2, 0), A1, rm("a2"), down)
-    mix((0, 0))
-    radd("p_z2o", rp("z2o"), (1, 0), B0)
-    rsend("p_z1o0", (1, 0), B0, rp("z1o0"), up)
-    radd("m_z2o", rm("z2o"), (-1, 0), B1)
-    rsend("m_z1o0", (-1, 0), B1, rm("z1o0"), down)
-    radd("p_z1y1", rp("z1y1"), (0, 1), B1)
-    radd("m_z1y1", rm("z1y1"), (0, 1), B0)
-    radd("ya1", RYA.at[1], (1, 0), A)
-    rsend("p_a1x", (1, 0), A1, rp("a1x"), up)
-    radd("p_z1y0", rp("z1y0"), (0, 1), B0)
-    radd("m_z1y0", rm("z1y0"), (0, 1), B1)
-    rsend("yb", (0, 1), B, RYB, over)
-    radd("ya2", RYA.at[2], (-1, 0), A)
-    rsend("m_a1x", (-1, 0), A0, rm("a1x"), down)
-    radd("p_a2", rp("a2"), (1, 0), A0)
-    rsend("p_a1y", (1, 0), A0, rp("a1y"), up)
-    radd("m_a2", rm("a2"), (-1, 0), A1)
-    rsend("m_a1y", (-1, 0), A1, rm("a1y"), down)
-
-    def total(part, *bufs):
-        value = sums((0, 0), part)[...].astype(F32)
-        for b in bufs:
-            value = value + b[...].astype(F32)
-        out_ref[rows_of(part), :] = value.astype(BF16)
-
-    arrived("r_ya3", RYA.at[3])
-    for name in ("z1o1", "z1o0"):
-        arrived("r_p_" + name, rp(name))
-        arrived("r_m_" + name, rm(name))
-    arrived("r_yb", RYB)
-    total(B0, rp("z1o0"), rm("z1o1"), cut(RYB, 0, 144))
-    total(B1, rp("z1o1"), rm("z1o0"), cut(RYB, 144, 144))
-    for name in ("a1x", "a1y"):
-        arrived("r_p_" + name, rp(name))
-        arrived("r_m_" + name, rm(name))
-    total(A0, cut(RYA.at[3], 0, 112), rp("a1y"), rm("a1x"))
-    total(A1, cut(RYA.at[3], 112, 112), rp("a1x"), rm("a1y"))
+    def across(k, w, d):
+        send("r%d_ya%d" % (w, k), sums(d, WAVES[w][2]), ya(k, w), over)
+
+    def open_wave(w):
+        A0, A1, A, B0, B1, B = WAVES[w]
+        mix(w, (2, 1))
+        across(0, w, (2, 1))
+        pass_on("pz2y", w, (2, 1), B0)
+        pass_on("mz2y", w, (2, 1), B1)
+        mix(w, (2, 0))
+        pass_on("pz2o", w, (2, 0), B0)
+        pass_on("mz2o", w, (2, 0), B1)
+        mix(w, (1, 1), (-1, 1))
+        across(1, w, (1, 1))
+        across(2, w, (-1, 1))
+        pass_on("pz1y1", w, (1, 1), B1)
+        pass_on("mz1y1", w, (-1, 1), B0)
+        mix(w, (0, 1))
+        across(3, w, (0, 1))
+        mix(w, (1, 0), (-1, 0))
+        pass_on("pz1o1", w, (1, 0), B1)
+        pass_on("mz1o1", w, (-1, 0), B0)
+        mix(w, (0, 0))
+
+    def early(w):
+        A0, A1, A, B0, B1, B = WAVES[w]
+        add("pz2y", w, (1, 1), B0)
+        pass_on("pz1y0", w, (1, 1), B0)
+        add("mz2y", w, (-1, 1), B1)
+        pass_on("mz1y0", w, (-1, 1), B1)
+        add("ya0", w, (2, 0), A, ya(0, w))
+        pass_on("pa2", w, (2, 0), A0)
+        pass_on("ma2", w, (2, 0), A1)
+        add("pz2o", w, (1, 0), B0)
+        pass_on("pz1o0", w, (1, 0), B0)
+        add("mz2o", w, (-1, 0), B1)
+        pass_on("mz1o0", w, (-1, 0), B1)
+
+    def middle(w):
+        A0, A1, A, B0, B1, B = WAVES[w]
+        add("pz1y1", w, (0, 1), B1)
+        add("mz1y1", w, (0, 1), B0)
+        add("ya1", w, (1, 0), A, ya(1, w))
+        pass_on("pa1x", w, (1, 0), A1)
+        add("ya2", w, (-1, 0), A, ya(2, w))
+        pass_on("ma1x", w, (-1, 0), A0)
+        add("pz1y0", w, (0, 1), B0)
+        add("mz1y0", w, (0, 1), B1)
+        send("r%d_yb" % w, sums((0, 1), B), yb(w), over)
+        add("pa2", w, (1, 0), A0)
+        pass_on("pa1y", w, (1, 0), A0)
+        add("ma2", w, (-1, 0), A1)
+        pass_on("ma1y", w, (-1, 0), A1)
+
+    def total(w, part, *bufs):
+        base, (start, size) = HALF * w, part
+        border = base + QUARTER
+        for lo_row, hi_row in ((start, min(start + size, border)), (max(start, border), start + size)):
+            if lo_row >= hi_row:
+                continue
+            n = hi_row - lo_row
+            value = sums((0, 0), (lo_row, n))[...].astype(F32)
+            for b in bufs:
+                value = value + cut(b, lo_row - start, n)[...].astype(F32)
+            u = lo_row - base
+            real = QUARTER * w + (u if u < QUARTER else u - QUARTER + HALF)
+            out_ref[pl.ds(real, n), :] = value.astype(BF16)
+
+    def close_wave(w):
+        A0, A1, A, B0, B1, B = WAVES[w]
+        arrived("r%d_ya3" % w, ya(3, w))
+        for name in ("pz1o1", "mz1o1", "pz1o0", "mz1o0"):
+            arrived("r%d_%s" % (w, name), inbox(name, w))
+        for name in ("pa1x", "ma1x", "pa1y", "ma1y"):
+            arrived("r%d_%s" % (w, name), inbox(name, w))
+        total(w, A0, cut(ya(3, w), 0, A0[1]), inbox("pa1y", w), inbox("ma1x", w))
+        total(w, A1, cut(ya(3, w), A0[1], A1[1]), inbox("pa1x", w), inbox("ma1y", w))
+        arrived("r%d_yb" % w, yb(w))
+        total(w, B0, inbox("pz1o0", w), inbox("mz1o1", w), cut(yb(w), 0, B0[1]))
+        total(w, B1, inbox("pz1o1", w), inbox("mz1o0", w), cut(yb(w), B0[1], B1[1]))
+
+    open_wave(0)
+    gate_wave(1)
+    gate_arrived(1)
+    open_wave(1)
+    early(0)
+    middle(0)
+    early(1)
+    close_wave(0)
+    middle(1)
+    close_wave(1)
     drain("")
 
 
@@ -519,18 +573,18 @@
             vm((CTX, HALF, 128), BF16),
             vm((CTX, HALF, 128), BF16),
             vm((CTX, HALF, 128), BF16),
-            vm((CTX, HALF, 128), BF16),
-            vm((CTX, HALF, 128), BF16),
+            vm((2, CTX, QUARTER, 128), BF16),
+            vm((2, CTX, QUARTER, 128), BF16),
             vm((16 * HALF, 128), BF16),
             vm((8, N, 128), F32),
             vm((16, N, 128), F32),
             vm((8, N, 128), F32),
             vm((N, N), BF16),
             vm((N, N), BF16),
-            vm((4, A[1], N), BF16),
-            vm((B[1], N), BF16),
-            vm((1200, N), BF16),
-            vm((1200, N), BF16),
+            vm((2, 4, 112, N), BF16),
+            vm((2, 160, N), BF16),
+            vm((1232, N), BF16),
+            vm((1216, N), BF16),
             pltpu.SemaphoreType.DMA((TRANSFERS,)),
             pltpu.SemaphoreType.DMA((TRANSFERS,)),
             pltpu.SemaphoreType.DMA((40,)),

time: 101 us -> 101 us (level)
  no operation moved by 1% of the time
where the time goes in v3:
time: 101 us; the launch traced here: 100 us
  Pallas kernels  99.7 us (99%)
    pallas_call x1, Pallas kernels, on_device(): pl.pallas_call(kernel, out_shape=pltpu.VMEM((N, N), BF16), in_specs=[anyw...  99.7 us

profile of v3, /device:TPU:1, one launch (start us, length us, event | category | flops | bytes accessed | tf_op | source)
XLA Modules:
  0.0 100.5 jit_solution(1785089480086184385)
XLA Ops:
  0.0 99.7 %hyena_block.1 = bf16[512,512]{1,0:T(8,128)(2,1)S(1)} custom-call(bf16[512,512]{1,0:T(8,128)(2,1)} %tok_hbm.1, bf16[8192,512]{1,0:T(8,128)(2,1)} %wv_hbm.1, bf16[8192,512]{1,0:T(8,128)(2,1)} %wg_hbm.1, bf16[512,512]{1,0:T(8,128)(2,1)} %filt_hbm.1, bf16[512,8192]{1,0:T(8,128)(2,1)} %wo_hbm.1, bf16[512,256]{1,0:T(8,128)(2,1)} %constant.4.clone.fwd_hbm, ...), custom_call_target="tpu_custom_call" | custom-call | tf_op jit(solution)/shard_map/hyena_block/pallas_call | solution.py:557
  99.7 0.8 copy.9
